TPU v7x, 32 devices: a whole 2x2x4 slice. The times are simulated.
32 devices in a mesh: docs: 4 (over y, x), wide: 8 (over z, core).
Axes of the slice: x: 2, y: 2, z: 4, core: 2. Of those that a mesh axis runs over, the one named last changes fastest.
Arguments:
- rows: bfloat16 [16384, 768], P(('docs', 'wide')), may hold values from -6 to 6
- cot_stream: float32 [16384, 768], P(('docs', 'wide')), may hold values from -6 to 6
- cot_joined: float32 [8192, 768], P(('docs', 'wide')), may hold values from -6 to 6
- page: int32 [16384], P(('docs', 'wide')), may hold values from -1 to 447, as said below
- key_mask: int32 [16384], P(('docs', 'wide')), may hold values 0 or 1
- w_qkv: float32 [2, 768, 2304], P(None, 'wide', 'docs'), may hold values from -0.21875 to 0.21875
- m_qkv: float32 [2, 768, 2304], P(None, 'wide', 'docs')
- v_qkv: float32 [2, 768, 2304], P(None, 'wide', 'docs'), as said below
- w_out: float32 [2, 768, 768], P(None, 'wide', 'docs'), may hold values from -0.875 to 0.875
- m_out: float32 [2, 768, 768], P(None, 'wide', 'docs')
- v_out: float32 [2, 768, 768], P(None, 'wide', 'docs'), as said below
- w_up: float32 [2, 768, 3072], P(None, 'wide', 'docs'), may hold values from -0.21875 to 0.21875
- m_up: float32 [2, 768, 3072], P(None, 'wide', 'docs')
- v_up: float32 [2, 768, 3072], P(None, 'wide', 'docs'), as said below
- w_down: float32 [2, 3072, 768], P(None, 'wide', 'docs'), may hold values from -0.109375 to 0.109375
- m_down: float32 [2, 3072, 768], P(None, 'wide', 'docs')
- v_down: float32 [2, 3072, 768], P(None, 'wide', 'docs'), as said below
- gains: float32 [5, 768], replicated
- m_gains: float32 [5, 768], replicated
- v_gains: float32 [5, 768], replicated, as said below
Outputs:
- stream_out: float32 [16384, 768], P(('docs', 'wide'))
- joined: float32 [8192, 768], P(('docs', 'wide'))
- grad_rows: float32 [16384, 768], P(('docs', 'wide'))
- new_w_qkv: float32 [2, 768, 2304], P(None, 'wide', 'docs')
- new_m_qkv: float32 [2, 768, 2304], P(None, 'wide', 'docs')
- new_v_qkv: float32 [2, 768, 2304], P(None, 'wide', 'docs')
- new_w_out: float32 [2, 768, 768], P(None, 'wide', 'docs')
- new_m_out: float32 [2, 768, 768], P(None, 'wide', 'docs')
- new_v_out: float32 [2, 768, 768], P(None, 'wide', 'docs')
- new_w_up: float32 [2, 768, 3072], P(None, 'wide', 'docs')
- new_m_up: float32 [2, 768, 3072], P(None, 'wide', 'docs')
- new_v_up: float32 [2, 768, 3072], P(None, 'wide', 'docs')
- new_w_down: float32 [2, 3072, 768], P(None, 'wide', 'docs')
- new_m_down: float32 [2, 3072, 768], P(None, 'wide', 'docs')
- new_v_down: float32 [2, 3072, 768], P(None, 'wide', 'docs')
- new_gains: float32 [5, 768], replicated
- new_m_gains: float32 [5, 768], replicated
- new_v_gains: float32 [5, 768], replicated
Inputs may be any that keep to these rules, and one draw needn't show every extreme that they name: Within each packed row pages are numbered from 0 in order, each at most 64 blocks, the first exactly 64; padding (-1) closes every packed row; the text and image rows of a block carry the same number; the largest page number is reached in every draw. `v_qkv`: second moments are positive. `v_out`: second moments are positive. `v_up`: second moments are positive. `v_down`: second moments are positive. `v_gains`: second moments are positive.
All inputs are finite; a program needn't handle non-finite values. No bound on the sum of `key_mask` on one device may be relied on, other than what follows from the above.
Results may differ from a plain program's by a relative error of at most 0.015.
The roundings to bfloat16 on the way count: a program that leaves them out, or rounds other values in their place, can miss the bound.
Values may be sent and summed in bfloat16 or wider, within the bound.
No kernel may reach another device: no remote copies, remote signals or barrier semaphores. Data moves between devices by JAX's collectives and lax.ppermute only.
A program may use at most 192 MiB of HBM per device.

v0:
```python
import jax
import jax.numpy as jnp
from jax import lax
from jax.sharding import PartitionSpec as P

HEADS = 12
STEP = 10


def from_behind(x, axis, by):
    count = lax.axis_size(axis)
    return lax.ppermute(x, axis, [(i, (i + by) % count) for i in range(count)])


def layer_norm(values, gain):
    centred = values - jnp.mean(values, axis=-1, keepdims=True)
    spread = jnp.mean(centred * centred, axis=-1, keepdims=True)
    return centred * lax.rsqrt(spread + 1e-05) * gain


def gelu_tanh(values):
    return jax.nn.gelu(values, approximate=True)


def adam_update(weight, first, second, grad, rate, decay):
    first_new = 0.9 * first + 0.1 * grad
    second_new = 0.999 * second + 0.001 * grad * grad
    first_hat = first_new / (1.0 - 0.9**STEP)
    second_hat = second_new / (1.0 - 0.999**STEP)
    weight_new = weight - rate * (first_hat / (jnp.sqrt(second_hat) + 1e-08) + decay * weight)
    return (weight_new, first_new, second_new)


def own_stream(piece, stream):
    return lax.dynamic_index_in_dim(piece, stream, 0, keepdims=False)


def placed_stream(piece, is_text):
    blank = jnp.zeros_like(piece)
    return jnp.where(is_text, jnp.stack((piece, blank)), jnp.stack((blank, piece)))


def fetch(w_qkv, w_out, w_up, w_down, stream):
    inner = (
        lax.all_gather(w_qkv.astype(jnp.bfloat16), "docs", axis=2, tiled=True),
        lax.all_gather(w_out.astype(jnp.bfloat16), "docs", axis=2, tiled=True),
        lax.all_gather(w_up.astype(jnp.bfloat16), "docs", axis=2, tiled=True),
        lax.all_gather(w_down.astype(jnp.bfloat16), "docs", axis=2, tiled=True),
    )
    whole = (
        lax.all_gather(inner[0], "wide", axis=1, tiled=True),
        lax.all_gather(inner[1], "wide", axis=1, tiled=True),
        lax.all_gather(inner[2], "wide", axis=1, tiled=True),
        lax.all_gather(inner[3], "wide", axis=1, tiled=True),
    )
    result = tuple((own_stream(piece, stream) for piece in whole))
    return result


def masked_scores(queries, key_rows, allowed, head_count, factor):
    count = queries.shape[0]
    raw = (
        jnp.einsum(
            "qhd,khd->hqk",
            queries.reshape(count, head_count, -1),
            key_rows.reshape(count, head_count, -1),
            preferred_element_type=jnp.float32,
        )
        * factor
    )
    return jnp.where(allowed[None], raw, -1000000000.0)


def shards(
    rows,
    cot_stream,
    cot_joined,
    page,
    key_mask,
    w_qkv,
    m_qkv,
    v_qkv,
    w_out,
    m_out,
    v_out,
    w_up,
    m_up,
    v_up,
    w_down,
    m_down,
    v_down,
    gains,
    m_gains,
    v_gains,
):
    half_size = lax.axis_size("wide") // 2
    stream = lax.axis_index("wide") // half_size
    is_text = stream == 0
    head_count = HEADS
    length = rows.shape[0]
    model_width = rows.shape[1]
    factor = float(model_width // head_count) ** (-0.5)
    qkv_low, out_low, up_low, down_low = fetch(w_qkv, w_out, w_up, w_down, stream)
    inputs = rows.astype(jnp.float32)
    valid_rows = (page >= 0).astype(jnp.float32)[:, None]
    gain_one = lax.dynamic_index_in_dim(gains, stream, 0, keepdims=False)
    gain_two = lax.dynamic_index_in_dim(gains, 2 + stream, 0, keepdims=False)
    gate_logit = gains[4]
    normed_one = layer_norm(inputs, gain_one).astype(jnp.bfloat16)
    projected = jnp.dot(normed_one, qkv_low, preferred_element_type=jnp.float32).astype(
        jnp.bfloat16
    )
    queries = projected[:, :model_width]
    own_kv = jnp.stack(
        (projected[:, model_width : 2 * model_width], projected[:, 2 * model_width :])
    )
    partner_kv = from_behind(own_kv, "wide", half_size)
    key_rows = partner_kv[0]
    value_heads = partner_kv[1].reshape(length, head_count, -1)
    position = lax.iota(jnp.int32, length)
    allowed = (page[:, None] == page[None, :]) & (
        (key_mask[None, :] == 1) | (position[:, None] == position[None, :])
    )
    scores = masked_scores(queries, key_rows, allowed, head_count, factor)
    row_top = jnp.max(scores, axis=-1, keepdims=True)
    log_total = row_top + jnp.log(jnp.sum(jnp.exp(scores - row_top), axis=-1, keepdims=True))
    probs_low = jnp.exp(scores - log_total).astype(jnp.bfloat16)
    attended = (
        jnp.einsum("hqk,khd->qhd", probs_low, value_heads, preferred_element_type=jnp.float32)
        .reshape(length, model_width)
        .astype(jnp.bfloat16)
    )
    branch = jnp.dot(attended, out_low, preferred_element_type=jnp.float32)
    middle = inputs + valid_rows * branch
    normed_two = layer_norm(middle, gain_two).astype(jnp.bfloat16)
    pre_act = jnp.dot(normed_two, up_low, preferred_element_type=jnp.float32)
    activated, gelu_back = jax.vjp(gelu_tanh, pre_act)
    acts_low = activated.astype(jnp.bfloat16)
    stream_out = middle + valid_rows * jnp.dot(
        acts_low, down_low, preferred_element_type=jnp.float32
    )
    half_rows = length // 2
    own_rows = lax.dynamic_slice_in_dim(stream_out, stream * half_rows, half_rows, 0)
    outgoing = lax.dynamic_slice_in_dim(stream_out, (1 - stream) * half_rows, half_rows, 0)
    partner_rows = from_behind(outgoing.astype(jnp.bfloat16), "wide", half_size).astype(
        outgoing.dtype
    )
    text_rows = jnp.where(is_text, own_rows, partner_rows)
    image_rows = jnp.where(is_text, partner_rows, own_rows)
    gate_mix = jax.nn.sigmoid(gate_logit)
    joined_rows = gate_mix * text_rows + (1.0 - gate_mix) * image_rows
    qkv_low, out_low, up_low, down_low = fetch(w_qkv, w_out, w_up, w_down, stream)
    gate_grad = jnp.sum(cot_joined * (text_rows - image_rows), axis=0) * gate_mix * (1.0 - gate_mix)
    text_grad = cot_joined * gate_mix
    image_grad = cot_joined * (1.0 - gate_mix)
    own_grad = jnp.where(is_text, text_grad, image_grad)
    other_grad = jnp.where(is_text, image_grad, text_grad)
    returned = from_behind(other_grad, "wide", half_size)
    upper_grad = jnp.where(is_text, own_grad, returned)
    lower_grad = jnp.where(is_text, returned, own_grad)
    out_grad = cot_stream + jnp.concatenate((upper_grad, lower_grad), axis=0)
    ffn_grad = (out_grad * valid_rows).astype(jnp.bfloat16)
    down_grad = jnp.dot(acts_low.T, ffn_grad, preferred_element_type=jnp.float32)
    acts_grad = jnp.dot(ffn_grad, down_low.T, preferred_element_type=jnp.float32)
    pre_grad = gelu_back(acts_grad)[0].astype(jnp.bfloat16)
    up_grad = jnp.dot(normed_two.T, pre_grad, preferred_element_type=jnp.float32)
    normed_two_grad = jnp.dot(pre_grad, up_low.T, preferred_element_type=jnp.float32)
    unused_two, norm_two_back = jax.vjp(layer_norm, middle, gain_two)
    middle_part, gain_two_grad = norm_two_back(normed_two_grad)
    middle_grad = out_grad + middle_part
    branch_grad = (middle_grad * valid_rows).astype(jnp.bfloat16)
    out_proj_grad = jnp.dot(attended.T, branch_grad, preferred_element_type=jnp.float32)
    attended_grad = jnp.dot(branch_grad, out_low.T, preferred_element_type=jnp.float32).astype(
        jnp.bfloat16
    )
    attended_grad = attended_grad.reshape(length, head_count, -1)
    probability = jnp.exp(masked_scores(queries, key_rows, allowed, head_count, factor) - log_total)
    probs_again = probability.astype(jnp.bfloat16)
    prob_grad = jnp.einsum(
        "qhd,khd->hqk", attended_grad, value_heads, preferred_element_type=jnp.float32
    )
    value_grad = jnp.einsum(
        "hqk,qhd->khd", probs_again, attended_grad, preferred_element_type=jnp.float32
    ).reshape(length, model_width)
    score_grad = (
        probability * (prob_grad - jnp.sum(prob_grad * probability, axis=-1, keepdims=True))
    ).astype(jnp.bfloat16)
    query_grad = (
        jnp.einsum(
            "hqk,khd->qhd",
            score_grad,
            key_rows.reshape(length, head_count, -1),
            preferred_element_type=jnp.float32,
        )
        * factor
    ).reshape(length, model_width)
    key_grad = (
        jnp.einsum(
            "hqk,qhd->khd",
            score_grad,
            queries.reshape(length, head_count, -1),
            preferred_element_type=jnp.float32,
        )
        * factor
    ).reshape(length, model_width)
    kv_grad = jnp.stack((key_grad, value_grad)).astype(jnp.bfloat16)
    own_kv_grad = from_behind(kv_grad, "wide", half_size)
    proj_grad = jnp.concatenate(
        (query_grad.astype(jnp.bfloat16), own_kv_grad[0], own_kv_grad[1]), axis=1
    )
    qkv_grad = jnp.dot(normed_one.T, proj_grad, preferred_element_type=jnp.float32)
    normed_one_grad = jnp.dot(proj_grad, qkv_low.T, preferred_element_type=jnp.float32)
    unused_one, norm_one_back = jax.vjp(layer_norm, inputs, gain_one)
    input_part, gain_one_grad = norm_one_back(normed_one_grad)
    grad_rows = middle_grad + input_part
    placed = tuple(
        (placed_stream(piece, is_text) for piece in (qkv_grad, out_proj_grad, up_grad, down_grad))
    )
    halves = (
        lax.psum_scatter(placed[0], "wide", scatter_dimension=1, tiled=True),
        lax.psum_scatter(placed[1], "wide", scatter_dimension=1, tiled=True),
        lax.psum_scatter(placed[2], "wide", scatter_dimension=1, tiled=True),
        lax.psum_scatter(placed[3], "wide", scatter_dimension=1, tiled=True),
    )
    reduced = (
        lax.psum_scatter(halves[0], "docs", scatter_dimension=2, tiled=True),
        lax.psum_scatter(halves[1], "docs", scatter_dimension=2, tiled=True),
        lax.psum_scatter(halves[2], "docs", scatter_dimension=2, tiled=True),
        lax.psum_scatter(halves[3], "docs", scatter_dimension=2, tiled=True),
    )
    slot_index = lax.iota(jnp.int32, 5)[:, None]
    small_terms = (
        jnp.where(slot_index == stream, gain_one_grad[None, :], 0.0)
        + jnp.where(slot_index == 2 + stream, gain_two_grad[None, :], 0.0)
        + jnp.where(slot_index == 4, gate_grad[None, :], 0.0)
    )
    gains_grad = lax.psum(small_terms, ("docs", "wide"))
    qkv_new = adam_update(w_qkv, m_qkv, v_qkv, reduced[0], 0.12, 0.01)
    out_new = adam_update(w_out, m_out, v_out, reduced[1], 0.5, 0.01)
    up_new = adam_update(w_up, m_up, v_up, reduced[2], 0.12, 0.01)
    down_new = adam_update(w_down, m_down, v_down, reduced[3], 0.06, 0.01)
    gains_new = adam_update(gains, m_gains, v_gains, gains_grad, 0.8, 0.0)
    return (
        stream_out,
        joined_rows,
        grad_rows,
        qkv_new[0],
        qkv_new[1],
        qkv_new[2],
        out_new[0],
        out_new[1],
        out_new[2],
        up_new[0],
        up_new[1],
        up_new[2],
        down_new[0],
        down_new[1],
        down_new[2],
        gains_new[0],
        gains_new[1],
        gains_new[2],
    )


def solution(mesh):
    return jax.shard_map(
        shards,
        mesh=mesh,
        in_specs=(
            P(("docs", "wide"), None),
            P(("docs", "wide"), None),
            P(("docs", "wide"), None),
            P(("docs", "wide")),
            P(("docs", "wide")),
            P(None, "wide", "docs"),
            P(None, "wide", "docs"),
            P(None, "wide", "docs"),
            P(None, "wide", "docs"),
            P(None, "wide", "docs"),
            P(None, "wide", "docs"),
            P(None, "wide", "docs"),
            P(None, "wide", "docs"),
            P(None, "wide", "docs"),
            P(None, "wide", "docs"),
            P(None, "wide", "docs"),
            P(None, "wide", "docs"),
            P(),
            P(),
            P(),
        ),
        out_specs=(
            P(("docs", "wide"), None),
            P(("docs", "wide"), None),
            P(("docs", "wide"), None),
            P(None, "wide", "docs"),
            P(None, "wide", "docs"),
            P(None, "wide", "docs"),
            P(None, "wide", "docs"),
            P(None, "wide", "docs"),
            P(None, "wide", "docs"),
            P(None, "wide", "docs"),
            P(None, "wide", "docs"),
            P(None, "wide", "docs"),
            P(None, "wide", "docs"),
            P(None, "wide", "docs"),
            P(None, "wide", "docs"),
            P(),
            P(),
            P(),
        ),
        check_vma=False,
    )
```

profile of v0, /device:TPU:0, one launch (start us, length us, event | category | flops | bytes accessed | tf_op | source)
XLA Modules:
  0.0 1354.6 jit_solution(5114454889149823214)
XLA Ops:
  12.3 19.2 %all_gather.32 = bf16[2,96,2304]{1,0,2:T(2,128)(2,1)S(1)} all-gather(bf16[2,96,576]{1,0,2:T(2,128)(2,1)S(1)} %copy.110), channel_id=1, replica_groups=mesh['docs'=4,'wide'=8] {'docs'}, dimensions={2}, use_global_device_ids=true | all-gather | bytes 1105920 | tf_op jit(solution)/shard_map/all_gather | solution.py:45
  34.1 12.6 all_gather.34
  48.5 29.0 %all-gather.15.cloned.1.call-done = bf16[2,384,768]{1,2,0:T(8,128)(2,1)} async-done(((bf16[2,384,192]{1,2,0:T(8,128)(2,1)}), bf16[2,384,768]{1,2,0:T(8,128)(2,1)}) %all-gather.15.cloned.1.call-update) | async-done | bytes 1179664 | tf_op jit(solution)/shard_map/all_gather | solution.py:48
  79.0 71.9 %all-gather.7.cloned.1.call-done = bf16[2,768,2304]{2,1,0:T(8,128)(2,1)} async-done(((bf16[2,96,2304]{2,1,0:T(8,128)(2,1)}), bf16[2,768,2304]{2,1,0:T(8,128)(2,1)}) %all-gather.7.cloned.1.call-update) | async-done | bytes 7077904 | tf_op jit(solution)/shard_map/all_gather | solution.py:51
  150.9 4.1 convolution_convert_fusion
  158.1 110.5 %collective-permute-done = bf16[2,512,768]{2,1,0:T(8,128)(2,1)} collective-permute-done((bf16[2,512,768]{2,1,0:T(8,128)(2,1)}, bf16[2,512,768]{2,1,0:T(8,128)(2,1)}, u32[]{:S(2)}, u32[]{:S(2)}) %collective-permute-start) | collective-permute-done | bytes 1572896 | tf_op jit(solution)/shard_map/ppermute | solution.py:12
  285.8 37.4 %all-gather.13.cloned.1.call-done = bf16[2,768,3072]{2,1,0:T(8,128)(2,1)} async-done(((bf16[2,96,3072]{2,1,0:T(8,128)(2,1)}), bf16[2,768,3072]{2,1,0:T(8,128)(2,1)}) %all-gather.13.cloned.1.call-update) | async-done | bytes 9437200 | tf_op jit(solution)/shard_map/all_gather | solution.py:53
  323.2 7.0 fusion.15
  330.2 85.2 %all-gather.17.cloned.1.call-done = bf16[2,3072,768]{1,2,0:T(8,128)(2,1)} async-done(((bf16[2,384,768]{1,2,0:T(8,128)(2,1)}), bf16[2,3072,768]{1,2,0:T(8,128)(2,1)}) %all-gather.17.cloned.1.call-update) | async-done | bytes 9437200 | tf_op jit(solution)/shard_map/all_gather | solution.py:54
  415.4 7.4 multiply_add_fusion
  425.0 18.2 %collective-permute-done.1 = bf16[256,768]{1,0:T(8,128)(2,1)S(1)} collective-permute-done((bf16[256,768]{1,0:T(8,128)(2,1)S(1)}, bf16[256,768]{1,0:T(8,128)(2,1)S(1)}, u32[]{:S(2)}, u32[]{:S(2)}) %collective-permute-start.1) | collective-permute-done | bytes 393248 | tf_op jit(solution)/shard_map/ppermute | solution.py:12
  444.7 36.0 %collective-permute-done.2 = f32[256,768]{1,0:T(8,128)S(1)} collective-permute-done((f32[256,768]{1,0:T(8,128)S(1)}, f32[256,768]{1,0:T(8,128)S(1)}, u32[]{:S(2)}, u32[]{:S(2)}) %collective-permute-start.2) | collective-permute-done | bytes 786464 | tf_op jit(solution)/shard_map/ppermute | solution.py:12
  484.1 7.9 fusion.8
  505.4 13.9 %multiply_reduce_fusion = (f32[12,512]{1,0:T(8,128)S(1)}, f32[12,512,512]{1,2,0:T(8,128)}) fusion(f32[12,512,512]{1,2,0:T(8,128)} %copy-done, f32[12,512]{1,0:T(8,128)S(1)} %log_add_fusion, pred[512,512]{0,1:T(8,128)(4,1)S(1)} %fusion.41, bf16[512,12,64]{0,2,1:T(8,128)(2,1)} %bitcast.92, bf16[512,12,64]{0,2,1:T(8,128)(2,1)} %bitcast.91), kind=kOutput, calls=%fused_computation.4 | convolution fusion | flops 418375680 | bytes 27049984 | tf_op jit(solution)/shard_map/qhd,khd->hqk/dot_general | solution.py:179
  519.4 7.4 multiply_convert_fusion
  535.3 86.0 %collective-permute-done.3 = bf16[2,512,768]{1,2,0:T(8,128)(2,1)S(1)} collective-permute-done((bf16[2,512,768]{1,2,0:T(8,128)(2,1)S(1)}, bf16[2,512,768]{1,2,0:T(8,128)(2,1)S(1)}, u32[]{:S(2)}, u32[]{:S(2)}) %collective-permute-start.3) | collective-permute-done | bytes 1572896 | tf_op jit(solution)/shard_map/ppermute | solution.py:12
  622.5 5.2 convolution_bitcast_fusion
  627.6 10.9 pad_select_fusion.2
  638.6 5.6 convolution_bitcast_fusion.1
  644.2 6.6 pad_select_fusion
  651.1 4.7 convolution_bitcast_fusion.2
  655.8 7.2 pad_select_fusion.1
  665.9 115.5 %reduce-scatter.12.cloned.1.call-done = f32[2,96,2304]{2,1,0:T(8,128)} async-done(((f32[2,768,2304]{2,1,0:T(8,128)}), f32[2,96,2304]{2,1,0:T(8,128)}) %reduce-scatter.12.cloned.1.call-update) | async-done | bytes 1769488 | tf_op jit(solution)/shard_map/reduce_scatter | solution.py:220
  781.4 4.1 copy.130
  789.6 180.5 %reduce-scatter.20.cloned.1.call-done = f32[2,384,768]{2,1,0:T(8,128)} async-done(((f32[2,3072,768]{2,1,0:T(8,128)}), f32[2,384,768]{2,1,0:T(8,128)}) %reduce-scatter.20.cloned.1.call-update) | async-done | bytes 2359312 | tf_op jit(solution)/shard_map/reduce_scatter | solution.py:223
  970.1 5.3 copy.122
  975.5 183.1 %reduce-scatter.16.cloned.1.call-done = f32[2,96,3072]{2,1,0:T(8,128)} async-done(((f32[2,768,3072]{2,1,0:T(8,128)}), f32[2,96,3072]{2,1,0:T(8,128)}) %reduce-scatter.16.cloned.1.call-update) | async-done | bytes 2359312 | tf_op jit(solution)/shard_map/reduce_scatter | solution.py:222
  1160.1 4.8 fusion.35
  1166.9 38.3 %psum.7 = f32[5,768]{1,0:T(8,128)S(1)} all-reduce(f32[5,768]{1,0:T(8,128)S(1)} %select_add_fusion), channel_id=1, replica_groups=mesh['docs'=4,'wide'=8] {'docs','wide'}, use_global_device_ids=true, to_apply=%region_22.23 | all-reduce | flops 3840 | bytes 30720 | tf_op jit(solution)/shard_map/psum | solution.py:237
  1211.3 16.0 %reduce-scatter.22.cloned.1.call-done = f32[576,192]{1,0:T(8,128)} async-done(((f32[2304,192]{1,0:T(8,128)}), f32[576,192]{1,0:T(8,128)}) %reduce-scatter.22.cloned.1.call-update) | async-done | bytes 442384
  1231.7 72.8 %all-reduce.11.cloned.1.call-done = f32[2,384,768]{1,0,2:T(2,128)} async-done(((f32[2,384,768]{1,0,2:T(2,128)}), f32[2,384,768]{1,0,2:T(2,128)}) %all-reduce.11.cloned.1.call-update) | async-done | bytes 2359312
  1307.3 37.8 %reduce-scatter.18.cloned.1.call-done = f32[2,96,768]{2,1,0:T(8,128)} async-done(((f32[2,96,3072]{2,1,0:T(8,128)}), f32[2,96,768]{2,1,0:T(8,128)}) %reduce-scatter.18.cloned.1.call-update) | async-done | bytes 589840 | tf_op jit(solution)/shard_map/reduce_scatter | solution.py:228
  (205 shorter events, 86.7 us)
Async XLA Ops:
  7.2 40.7 %all-gather.11.cloned.1.call-start = ((), (), s32[]{:S(2)}) async-start(), calls=%async_computation.9 | async-start | bytes 1474560 | tf_op jit(solution)/shard_map/all_gather | solution.py:47
  9.1 68.3 %all-gather.15.cloned.1.call-start = ((), (), s32[]{:S(2)}) async-start(), calls=%async_computation.11 | async-start | bytes 1474560 | tf_op jit(solution)/shard_map/all_gather | solution.py:48
  11.0 139.9 %all-gather.7.cloned.1.call-start = ((), (), s32[]{:S(2)}) async-start(), calls=%async_computation.7 | async-start | bytes 7962624 | tf_op jit(solution)/shard_map/all_gather | solution.py:51
  33.9 249.1 %all-gather.9.cloned.1.call-start = ((), (), s32[]{:S(2)}) async-start(), calls=%async_computation.8 | async-start | bytes 2654208 | tf_op jit(solution)/shard_map/all_gather | solution.py:52
  47.8 275.4 %all-gather.13.cloned.1.call-start = ((), (), s32[]{:S(2)}) async-start(), calls=%async_computation.10 | async-start | bytes 10616832 | tf_op jit(solution)/shard_map/all_gather | solution.py:53
  48.4 367.0 %all-gather.17.cloned.1.call-start = ((), (), s32[]{:S(2)}) async-start(), calls=%async_computation.12 | async-start | bytes 10616832 | tf_op jit(solution)/shard_map/all_gather | solution.py:54
  77.4 585.6 %reduce-scatter.14.cloned.1.call-start = ((), (), s32[]{:S(2)}) async-start(), calls=%async_computation.14 | async-start | bytes 5308416 | tf_op jit(solution)/shard_map/reduce_scatter | solution.py:221
  78.1 76.9 %copy-start.37 = (f32[512]{0:T(512)}, f32[512]{0:T(512)S(1)}, u32[]{:S(2)}) copy-start(f32[512]{0:T(512)S(1)} %fusion.34) | copy-start | bytes 6148
  156.5 112.2 %collective-permute-start = (bf16[2,512,768]{2,1,0:T(8,128)(2,1)}, bf16[2,512,768]{2,1,0:T(8,128)(2,1)}, u32[]{:S(2)}, u32[]{:S(2)}) collective-permute-start(bf16[2,512,768]{2,1,0:T(8,128)(2,1)} %pad_maximum_fusion.1), channel_id=1, source_target_pairs={{0,4},{1,5},{2,6},{3,7},{4,0},{5,1},{6,2},{7,3},{8,12},{9,13},{10,... | collective-permute-start | bytes 4718600 | tf_op jit(solution)/shard_map/ppermute | solution.py:12
  158.1 114.9 %copy-start.6 = (bf16[512,768]{0,1:T(8,128)(2,1)}, bf16[512,768]{0,1:T(8,128)(2,1)S(1)}, u32[]{:S(2)}) copy-start(bf16[512,768]{0,1:T(8,128)(2,1)S(1)} %copy.113) | copy-start | bytes 2359300
  330.2 113.0 %copy-start.8 = (f32[256,768]{1,0:T(8,128)S(1)}, f32[256,768]{1,0:T(8,128)}, u32[]{:S(2)}) copy-start(f32[256,768]{1,0:T(8,128)} %param.22) | copy-start | bytes 2359300
  424.0 19.2 %collective-permute-start.1 = (bf16[256,768]{1,0:T(8,128)(2,1)S(1)}, bf16[256,768]{1,0:T(8,128)(2,1)S(1)}, u32[]{:S(2)}, u32[]{:S(2)}) collective-permute-start(bf16[256,768]{1,0:T(8,128)(2,1)S(1)} %dynamic-slice_convert_fusion), channel_id=1, source_target_pairs={{0,4},{1,5},{2,6},{3,7},{4,0},{5,1},{6,2},{7,3},{8,12},{9,13},{10,... | collective-permute-start | bytes 1179656 | tf_op jit(solution)/shard_map/ppermute | solution.py:12
  425.0 55.7 %copy-start.17 = (f32[512,768]{1,0:T(8,128)S(1)}, f32[512,768]{1,0:T(8,128)}, u32[]{:S(2)}) copy-start(f32[512,768]{1,0:T(8,128)} %copy-done.16) | copy-start | bytes 4718596
  444.7 36.0 %collective-permute-start.2 = (f32[256,768]{1,0:T(8,128)S(1)}, f32[256,768]{1,0:T(8,128)S(1)}, u32[]{:S(2)}, u32[]{:S(2)}) collective-permute-start(f32[256,768]{1,0:T(8,128)S(1)} %multiply_select_fusion.1), channel_id=1, source_target_pairs={{0,4},{1,5},{2,6},{3,7},{4,0},{5,1},{6,2},{7,3},{8,12},{9,13},{10,... | collective-permute-start | bytes 2359304 | tf_op jit(solution)/shard_map/ppermute | solution.py:12
  500.1 281.4 %reduce-scatter.12.cloned.1.call-start = ((), (), s32[]{:S(2)}) async-start(), calls=%async_computation.13 | async-start | bytes 15925248 | tf_op jit(solution)/shard_map/reduce_scatter | solution.py:220
  534.0 87.2 %collective-permute-start.3 = (bf16[2,512,768]{1,2,0:T(8,128)(2,1)S(1)}, bf16[2,512,768]{1,2,0:T(8,128)(2,1)S(1)}, u32[]{:S(2)}, u32[]{:S(2)}) collective-permute-start(bf16[2,512,768]{1,2,0:T(8,128)(2,1)S(1)} %pad_maximum_fusion.2), channel_id=1, source_target_pairs={{0,4},{1,5},{2,6},{3,7},{4,0},{5,1},{6,2},{7,3},{8,12},{9,13},{10,... | collective-permute-start | bytes 4718600 | tf_op jit(solution)/shard_map/ppermute | solution.py:12
  535.3 86.1 %copy-start.14 = (bf16[12,64,512]{2,1,0:T(8,128)(2,1)}, bf16[12,64,512]{2,1,0:T(8,128)(2,1)S(1)}, u32[]{:S(2)}) copy-start(bf16[12,64,512]{2,1,0:T(8,128)(2,1)S(1)} %multiply_convert_fusion.3) | copy-start | bytes 2359300
  535.3 87.2 %copy-start.2 = (bf16[512,768]{1,0:T(8,128)(2,1)S(1)}, bf16[512,768]{1,0:T(8,128)(2,1)}, u32[]{:S(2)}) copy-start(bf16[512,768]{1,0:T(8,128)(2,1)} %param.20) | copy-start | bytes 2359300
  638.6 331.5 %reduce-scatter.20.cloned.1.call-start = ((), (), s32[]{:S(2)}) async-start(), calls=%async_computation.17 | async-start | bytes 21233664 | tf_op jit(solution)/shard_map/reduce_scatter | solution.py:223
  650.9 507.8 %reduce-scatter.16.cloned.1.call-start = ((), (), s32[]{:S(2)}) async-start(), calls=%async_computation.15 | async-start | bytes 21233664 | tf_op jit(solution)/shard_map/reduce_scatter | solution.py:222
  663.0 546.1 %reduce-scatter.24.cloned.1.call-start = ((), (), s32[]{:S(2)}) async-start(), calls=%async_computation.19 | async-start | bytes 983040
  665.9 561.5 %reduce-scatter.22.cloned.1.call-start = ((), (), s32[]{:S(2)}) async-start(), calls=%async_computation.18 | async-start | bytes 2949120
  789.5 515.0 %all-reduce.11.cloned.1.call-start = ((), (), s32[]{:S(2)}) async-start(), calls=%async_computation.20 | async-start | bytes 4718592
  975.5 183.2 %copy-start.40 = (u32[32]{0:T(128)S(1)}, u32[32]{0:T(128)}, u32[]{:S(2)}) copy-start(u32[32]{0:T(128)} %constant.188) | copy-start | bytes 388
  975.5 184.5 %copy-start.3 = (bf16[512,768]{1,0:T(8,128)(2,1)S(1)}, bf16[512,768]{1,0:T(8,128)(2,1)}, u32[]{:S(2)}) copy-start(bf16[512,768]{1,0:T(8,128)(2,1)} %param.20) | copy-start | bytes 2359300
  975.5 184.5 %copy-start.15 = (bf16[12,64,512]{2,1,0:T(8,128)(2,1)S(1)}, bf16[12,64,512]{2,1,0:T(8,128)(2,1)}, u32[]{:S(2)}) copy-start(bf16[12,64,512]{2,1,0:T(8,128)(2,1)} %copy-done.14) | copy-start | bytes 2359300
  975.5 369.6 %reduce-scatter.18.cloned.1.call-start = ((), (), s32[]{:S(2)}) async-start(), calls=%async_computation.16 | async-start | bytes 2949120 | tf_op jit(solution)/shard_map/reduce_scatter | solution.py:228
  1228.8 77.0 %copy-start.18 = (f32[2,384,192]{1,2,0:T(8,128)S(1)}, f32[2,384,192]{1,2,0:T(8,128)}, u32[]{:S(2)}) copy-start(f32[2,384,192]{1,2,0:T(8,128)} %param.34) | copy-start | bytes 1769476
  1228.8 77.0 %copy-start.28 = (f32[2,384,192]{1,2,0:T(8,128)S(1)}, f32[2,384,192]{1,2,0:T(8,128)}, u32[]{:S(2)}) copy-start(f32[2,384,192]{1,2,0:T(8,128)} %param.35) | copy-start | bytes 1769476
  1228.8 77.0 %copy-start.29 = (f32[2,384,192]{1,2,0:T(8,128)S(1)}, f32[2,384,192]{1,2,0:T(8,128)}, u32[]{:S(2)}) copy-start(f32[2,384,192]{1,2,0:T(8,128)} %param.36) | copy-start | bytes 1769476
  1231.7 113.4 %copy-start.19 = (f32[2,96,768]{2,1,0:T(8,128)S(1)}, f32[2,96,768]{2,1,0:T(8,128)}, u32[]{:S(2)}) copy-start(f32[2,96,768]{2,1,0:T(8,128)} %param.31) | copy-start | bytes 1769476
  1231.7 113.4 %copy-start.30 = (f32[2,96,768]{2,1,0:T(8,128)S(1)}, f32[2,96,768]{2,1,0:T(8,128)}, u32[]{:S(2)}) copy-start(f32[2,96,768]{2,1,0:T(8,128)} %param.32) | copy-start | bytes 1769476
  (34 other events, 392.5 us)
Sparse Core Ops, SparseCore 0:
  10.4 36.4 all-gather.10
  49.3 28.0 all-gather.14
  79.6 71.2 all-gather.6
  152.9 69.7 all-gather.8
  224.1 99.0 all-gather.12
  324.7 90.7 all-gather.16
  500.2 71.2 reduce-scatter.13
  638.7 142.6 reduce-scatter.11
  783.8 186.2 reduce-scatter.19
  972.3 186.3 reduce-scatter.15
  1161.6 24.7 reduce-scatter.23
  1189.3 37.9 reduce-scatter.21
  1230.5 74.0 all-reduce.10
  1307.7 37.3 reduce-scatter.17
where the time goes:
time: 1360 us; the launch traced here: 1350 us
  waiting for transfers between devices  1080 us (79%)
  matrix products  82.1 us (6%)
  blocking collectives  70.1 us (5%)
  other arithmetic  63 us (5%)
  local copies, waits for them, and re-layouts  40.1 us (3%)
  between operations  15.7 us (1%)
    ppermute x4, waiting for transfers between devices, from_behind(): return lax.ppermute(x, axis, [(i, (i + by) % count) for i in range(count)])  251 us
    reduce_scatter x1, waiting for transfers between devices, shards(): lax.psum_scatter(placed[2], 'wide', scatter_dimension=1, tiled=True)  183 us
    reduce_scatter x1, waiting for transfers between devices, shards(): lax.psum_scatter(placed[3], 'wide', scatter_dimension=1, tiled=True)  181 us
    reduce_scatter x1, waiting for transfers between devices, shards(): lax.psum_scatter(placed[0], 'wide', scatter_dimension=1, tiled=True)  116 us
    unnamed x17, waiting for transfers between devices  89.5 us
    all_gather x1, waiting for transfers between devices, fetch(): lax.all_gather(inner[3], 'wide', axis=1, tiled=True)  85.2 us
    all_gather x1, waiting for transfers between devices, fetch(): lax.all_gather(inner[0], 'wide', axis=1, tiled=True)  71.9 us
    psum x1, blocking collectives, shards(): gains_grad = lax.psum(small_terms, ('docs', 'wide'))  38.3 us
  transfers between devices with their start and end apart: 18, of which 14 were waited for; matrix products, arithmetic and copies ran while one was open for 11% of the time, Pallas kernels for 0%

commit v1 on v0

--- a/solution.py
+++ b/solution.py
@@ -5,6 +5,18 @@
 
 HEADS = 12
 STEP = 10
+
+
+def collect(value, axis, dim):
+    ways, here, step = (lax.axis_size(axis), lax.axis_index(axis), value.shape[dim])
+    line, have = (value, 1)
+    while have < ways:
+        line = jnp.concatenate(
+            [line, lax.ppermute(line, axis, [(d, (d - have) % ways) for d in range(ways)])],
+            axis=dim,
+        )
+        have = 2 * have
+    return jnp.roll(line, here * step, axis=dim)
 
 
 def from_behind(x, axis, by):
@@ -48,7 +60,7 @@
         lax.all_gather(w_down.astype(jnp.bfloat16), "docs", axis=2, tiled=True),
     )
     whole = (
-        lax.all_gather(inner[0], "wide", axis=1, tiled=True),
+        collect(inner[0], "wide", 1),
         lax.all_gather(inner[1], "wide", axis=1, tiled=True),
         lax.all_gather(inner[2], "wide", axis=1, tiled=True),
         lax.all_gather(inner[3], "wide", axis=1, tiled=True),

time: 1360 us -> 1510 us (1.11)
  waiting for transfers between devices: 1080 us -> 1220 us
    ppermute x0 -> x3, waiting for transfers between devices: none -> 359 us  [collect(): lax.ppermute(line, axis, [(d, (d - have) % ways) for d in range(ways)])]
    all_gather x1, waiting for transfers between devices: 85.2 us -> 0.01 us  [fetch(): lax.all_gather(inner[3], 'wide', axis=1, tiled=True)]
    all_gather x1 -> x0, waiting for transfers between devices: 71.9 us -> none  [fetch(): lax.all_gather(inner[0], 'wide', axis=1, tiled=True)]
    ppermute x4, waiting for transfers between devices: 251 us -> 212 us  [from_behind(): return lax.ppermute(x, axis, [(i, (i + by) % count) for i in range(count)])]
    all_gather x1, waiting for transfers between devices: 37.4 us -> 0.02 us  [fetch(): lax.all_gather(inner[2], 'wide', axis=1, tiled=True)]
    all_gather x1, waiting for transfers between devices: 0.02 us -> 15.8 us  [fetch(): lax.all_gather(w_up.astype(jnp.bfloat16), 'docs', axis=2, tiled=True)]
    concatenate x0 -> x3, other arithmetic: none -> 15.4 us  [the longest x1 13.4 us: collect(): return jnp.roll(line, here * step, axis=dim)]
    unnamed x17 -> x16, waiting for transfers between devices: 89.5 us -> 88.9 us
  transfers between devices with their start and end apart: 18 -> 20, of which waited for: 14 -> 15; matrix products, arithmetic and copies ran while one was open for 11% -> 10% of each run, Pallas kernels for 0% -> 0%
where the time goes in v1:
time: 1510 us; the launch traced here: 1500 us
  waiting for transfers between devices  1220 us (81%)
  matrix products  80.3 us (5%)
  other arithmetic  75.7 us (5%)
  blocking collectives  64.9 us (4%)
  local copies, waits for them, and re-layouts  37.8 us (3%)
  between operations  15.9 us (1%)
    ppermute x3, waiting for transfers between devices, collect(): lax.ppermute(line, axis, [(d, (d - have) % ways) for d in range(ways)])  359 us
    ppermute x4, waiting for transfers between devices, from_behind(): return lax.ppermute(x, axis, [(i, (i + by) % count) for i in range(count)])  212 us
    reduce_scatter x1, waiting for transfers between devices, shards(): lax.psum_scatter(placed[2], 'wide', scatter_dimension=1, tiled=True)  183 us
    reduce_scatter x1, waiting for transfers between devices, shards(): lax.psum_scatter(placed[3], 'wide', scatter_dimension=1, tiled=True)  181 us
    reduce_scatter x1, waiting for transfers between devices, shards(): lax.psum_scatter(placed[0], 'wide', scatter_dimension=1, tiled=True)  115 us
    unnamed x16, waiting for transfers between devices  88.9 us
    psum x1, blocking collectives, shards(): gains_grad = lax.psum(small_terms, ('docs', 'wide'))  38.4 us
    reduce_scatter x1, waiting for transfers between devices, shards(): lax.psum_scatter(halves[2], 'docs', scatter_dimension=2, tiled=True)  38 us
  transfers between devices with their start and end apart: 20, of which 15 were waited for; matrix products, arithmetic and copies ran while one was open for 10% of the time, Pallas kernels for 0%

profile of v1, /device:TPU:0, one launch (start us, length us, event | category | flops | bytes accessed | tf_op | source)
XLA Modules:
  0.0 1504.5 jit_solution(13381899062424121451)
XLA Ops:
  12.1 12.0 all_gather.29
  25.2 15.8 %all-gather.8.cloned.1.call-done = bf16[2,96,3072]{2,1,0:T(8,128)(2,1)} async-done(((bf16[2,96,768]{2,1,0:T(8,128)(2,1)}), bf16[2,96,3072]{2,1,0:T(8,128)(2,1)}) %all-gather.8.cloned.1.call-update) | async-done | bytes 1179664 | tf_op jit(solution)/shard_map/all_gather | solution.py:59
  41.0 30.1 %all-gather.12.cloned.1.call-done = bf16[2,384,768]{1,2,0:T(8,128)(2,1)} async-done(((bf16[2,384,192]{1,2,0:T(8,128)(2,1)}), bf16[2,384,768]{1,2,0:T(8,128)(2,1)}) %all-gather.12.cloned.1.call-update) | async-done | bytes 1179664 | tf_op jit(solution)/shard_map/all_gather | solution.py:60
  71.5 14.5 all_gather.28
  89.0 20.8 %collective-permute-done = bf16[2,96,2304]{2,1,0:T(8,128)(2,1)S(1)} collective-permute-done((bf16[2,96,2304]{2,1,0:T(8,128)(2,1)S(1)}, bf16[2,96,2304]{2,1,0:T(8,128)(2,1)S(1)}, u32[]{:S(2)}, u32[]{:S(2)}) %collective-permute-start) | collective-permute-done | bytes 884768 | tf_op jit(solution)/shard_map/ppermute | solution.py:15
  113.6 87.8 %collective-permute-done.1 = bf16[2,192,2304]{2,1,0:T(8,128)(2,1)S(1)} collective-permute-done((bf16[2,192,2304]{2,1,0:T(8,128)(2,1)S(1)}, bf16[2,192,2304]{2,1,0:T(8,128)(2,1)S(1)}, u32[]{:S(2)}, u32[]{:S(2)}) %collective-permute-start.1) | collective-permute-done | bytes 1769504 | tf_op jit(solution)/shard_map/ppermute | solution.py:15
  205.9 249.9 %collective-permute-done.2 = bf16[2,384,2304]{2,1,0:T(8,128)(2,1)} collective-permute-done((bf16[2,384,2304]{2,1,0:T(8,128)(2,1)}, bf16[2,384,2304]{2,1,0:T(8,128)(2,1)}, u32[]{:S(2)}, u32[]{:S(2)}) %collective-permute-start.2) | collective-permute-done | bytes 3538976 | tf_op jit(solution)/shard_map/ppermute | solution.py:15
  455.9 13.4 fusion.24
  472.7 70.8 %collective-permute-done.3 = bf16[2,512,768]{2,1,0:T(8,128)(2,1)} collective-permute-done((bf16[2,512,768]{2,1,0:T(8,128)(2,1)S(1)}, bf16[2,512,768]{2,1,0:T(8,128)(2,1)}, u32[]{:S(2)}, u32[]{:S(2)}) %collective-permute-start.3) | collective-permute-done | bytes 1572896 | tf_op jit(solution)/shard_map/ppermute | solution.py:24
  558.3 7.5 fusion.15
  565.8 7.4 multiply_add_fusion
  574.5 19.0 %collective-permute-done.4 = bf16[256,768]{1,0:T(8,128)(2,1)S(1)} collective-permute-done((bf16[256,768]{1,0:T(8,128)(2,1)S(1)}, bf16[256,768]{1,0:T(8,128)(2,1)S(1)}, u32[]{:S(2)}, u32[]{:S(2)}) %collective-permute-start.4) | collective-permute-done | bytes 393248 | tf_op jit(solution)/shard_map/ppermute | solution.py:24
  595.0 37.0 %collective-permute-done.5 = f32[256,768]{1,0:T(8,128)S(1)} collective-permute-done((f32[256,768]{1,0:T(8,128)S(1)}, f32[256,768]{1,0:T(8,128)S(1)}, u32[]{:S(2)}, u32[]{:S(2)}) %collective-permute-start.5) | collective-permute-done | bytes 786464 | tf_op jit(solution)/shard_map/ppermute | solution.py:24
  634.4 7.8 fusion.8
  655.9 13.7 multiply_reduce_fusion
  669.6 7.1 multiply_convert_fusion
  685.1 85.5 %collective-permute-done.6 = bf16[2,512,768]{1,2,0:T(8,128)(2,1)S(1)} collective-permute-done((bf16[2,512,768]{1,2,0:T(8,128)(2,1)S(1)}, bf16[2,512,768]{1,2,0:T(8,128)(2,1)S(1)}, u32[]{:S(2)}, u32[]{:S(2)}) %collective-permute-start.6) | collective-permute-done | bytes 1572896 | tf_op jit(solution)/shard_map/ppermute | solution.py:24
  771.9 5.2 convolution_bitcast_fusion
  777.1 11.0 pad_select_fusion.2
  788.2 5.6 convolution_bitcast_fusion.1
  793.8 6.6 pad_select_fusion
  800.7 4.7 convolution_bitcast_fusion.2
  805.4 7.1 pad_select_fusion.1
  815.5 115.5 %reduce-scatter.12.cloned.1.call-done = f32[2,96,2304]{2,1,0:T(8,128)} async-done(((f32[2,768,2304]{2,1,0:T(8,128)}), f32[2,96,2304]{2,1,0:T(8,128)}) %reduce-scatter.12.cloned.1.call-update) | async-done | bytes 1769488 | tf_op jit(solution)/shard_map/reduce_scatter | solution.py:232
  939.1 180.6 %reduce-scatter.20.cloned.1.call-done = f32[2,384,768]{2,1,0:T(8,128)} async-done(((f32[2,3072,768]{2,1,0:T(8,128)}), f32[2,384,768]{2,1,0:T(8,128)}) %reduce-scatter.20.cloned.1.call-update) | async-done | bytes 2359312 | tf_op jit(solution)/shard_map/reduce_scatter | solution.py:235
  1119.7 5.3 copy.128
  1125.1 183.3 %reduce-scatter.16.cloned.1.call-done = f32[2,96,3072]{2,1,0:T(8,128)} async-done(((f32[2,768,3072]{2,1,0:T(8,128)}), f32[2,96,3072]{2,1,0:T(8,128)}) %reduce-scatter.16.cloned.1.call-update) | async-done | bytes 2359312 | tf_op jit(solution)/shard_map/reduce_scatter | solution.py:234
  1309.8 4.8 fusion.40
  1316.6 38.4 %psum.7 = f32[5,768]{1,0:T(8,128)S(1)} all-reduce(f32[5,768]{1,0:T(8,128)S(1)} %select_add_fusion), channel_id=1, replica_groups=mesh['docs'=4,'wide'=8] {'docs','wide'}, use_global_device_ids=true, to_apply=%region_22.24 | all-reduce | flops 3840 | bytes 30720 | tf_op jit(solution)/shard_map/psum | solution.py:249
  1361.1 15.9 %reduce-scatter.22.cloned.1.call-done = f32[576,192]{1,0:T(8,128)} async-done(((f32[2304,192]{1,0:T(8,128)}), f32[576,192]{1,0:T(8,128)}) %reduce-scatter.22.cloned.1.call-update) | async-done | bytes 442384
  1381.3 72.8 %all-reduce.11.cloned.1.call-done = f32[2,384,768]{1,0,2:T(2,128)} async-done(((f32[2,384,768]{1,0,2:T(2,128)}), f32[2,384,768]{1,0,2:T(2,128)}) %all-reduce.11.cloned.1.call-update) | async-done | bytes 2359312
  1456.8 38.0 %reduce-scatter.18.cloned.1.call-done = f32[2,96,768]{2,1,0:T(8,128)} async-done(((f32[2,96,3072]{2,1,0:T(8,128)}), f32[2,96,768]{2,1,0:T(8,128)}) %reduce-scatter.18.cloned.1.call-update) | async-done | bytes 589840 | tf_op jit(solution)/shard_map/reduce_scatter | solution.py:240
  (217 shorter events, 93.8 us)
Async XLA Ops:
  7.2 33.8 %all-gather.8.cloned.1.call-start = ((), (), s32[]{:S(2)}) async-start(), calls=%async_computation.8 | async-start | bytes 1474560 | tf_op jit(solution)/shard_map/all_gather | solution.py:59
  9.1 62.0 %all-gather.12.cloned.1.call-start = ((), (), s32[]{:S(2)}) async-start(), calls=%async_computation.10 | async-start | bytes 1474560 | tf_op jit(solution)/shard_map/all_gather | solution.py:60
  11.0 544.5 %all-gather.6.cloned.1.call-start = ((), (), s32[]{:S(2)}) async-start(), calls=%async_computation.7 | async-start | bytes 2654208 | tf_op jit(solution)/shard_map/all_gather | solution.py:64
  25.1 533.2 %all-gather.10.cloned.1.call-start = ((), (), s32[]{:S(2)}) async-start(), calls=%async_computation.9 | async-start | bytes 10616832 | tf_op jit(solution)/shard_map/all_gather | solution.py:65
  41.0 524.8 %all-gather.14.cloned.1.call-start = ((), (), s32[]{:S(2)}) async-start(), calls=%async_computation.11 | async-start | bytes 10616832 | tf_op jit(solution)/shard_map/all_gather | solution.py:66
  71.2 741.4 %reduce-scatter.14.cloned.1.call-start = ((), (), s32[]{:S(2)}) async-start(), calls=%async_computation.13 | async-start | bytes 5308416 | tf_op jit(solution)/shard_map/reduce_scatter | solution.py:233
  87.6 22.2 %collective-permute-start = (bf16[2,96,2304]{2,1,0:T(8,128)(2,1)S(1)}, bf16[2,96,2304]{2,1,0:T(8,128)(2,1)S(1)}, u32[]{:S(2)}, u32[]{:S(2)}) collective-permute-start(bf16[2,96,2304]{2,1,0:T(8,128)(2,1)S(1)} %copy.117), channel_id=1, source_target_pairs={{0,7},{1,0},{2,1},{3,2},{4,3},{5,4},{6,5},{7,6},{8,15},{9,8},{10,9... | collective-permute-start | bytes 2654216 | tf_op jit(solution)/shard_map/ppermute | solution.py:15
  110.0 94.5 %copy-start.1 = (bf16[512,768]{1,0:T(8,128)(2,1)S(1)}, bf16[512,768]{1,0:T(8,128)(2,1)}, u32[]{:S(2)}) copy-start(bf16[512,768]{1,0:T(8,128)(2,1)} %param.22) | copy-start | bytes 2359300
  110.0 91.4 %collective-permute-start.1 = (bf16[2,192,2304]{2,1,0:T(8,128)(2,1)S(1)}, bf16[2,192,2304]{2,1,0:T(8,128)(2,1)S(1)}, u32[]{:S(2)}, u32[]{:S(2)}) collective-permute-start(bf16[2,192,2304]{2,1,0:T(8,128)(2,1)S(1)} %pad_maximum_fusion.2), channel_id=1, source_target_pairs={{0,6},{1,7},{2,0},{3,1},{4,2},{5,3},{6,4},{7,5},{8,14},{9,15},{10,... | collective-permute-start | bytes 5308424 | tf_op jit(solution)/shard_map/ppermute | solution.py:15
  203.8 252.1 %collective-permute-start.2 = (bf16[2,384,2304]{2,1,0:T(8,128)(2,1)}, bf16[2,384,2304]{2,1,0:T(8,128)(2,1)}, u32[]{:S(2)}, u32[]{:S(2)}) collective-permute-start(bf16[2,384,2304]{2,1,0:T(8,128)(2,1)} %pad_maximum_fusion), channel_id=1, source_target_pairs={{0,4},{1,5},{2,6},{3,7},{4,0},{5,1},{6,2},{7,3},{8,12},{9,13},{10,... | collective-permute-start | bytes 10616840 | tf_op jit(solution)/shard_map/ppermute | solution.py:15
  205.0 264.3 %copy-start.40 = (f32[512]{0:T(512)}, f32[512]{0:T(512)S(1)}, u32[]{:S(2)}) copy-start(f32[512]{0:T(512)S(1)} %fusion.39) | copy-start | bytes 6148
  471.8 71.7 %collective-permute-start.3 = (bf16[2,512,768]{2,1,0:T(8,128)(2,1)S(1)}, bf16[2,512,768]{2,1,0:T(8,128)(2,1)}, u32[]{:S(2)}, u32[]{:S(2)}) collective-permute-start(bf16[2,512,768]{2,1,0:T(8,128)(2,1)S(1)} %pad_maximum_fusion.3), channel_id=1, source_target_pairs={{0,4},{1,5},{2,6},{3,7},{4,0},{5,1},{6,2},{7,3},{8,12},{9,13},{10,... | collective-permute-start | bytes 4718600 | tf_op jit(solution)/shard_map/ppermute | solution.py:24
  574.4 19.1 %collective-permute-start.4 = (bf16[256,768]{1,0:T(8,128)(2,1)S(1)}, bf16[256,768]{1,0:T(8,128)(2,1)S(1)}, u32[]{:S(2)}, u32[]{:S(2)}) collective-permute-start(bf16[256,768]{1,0:T(8,128)(2,1)S(1)} %dynamic-slice_convert_fusion), channel_id=1, source_target_pairs={{0,4},{1,5},{2,6},{3,7},{4,0},{5,1},{6,2},{7,3},{8,12},{9,13},{10,... | collective-permute-start | bytes 1179656 | tf_op jit(solution)/shard_map/ppermute | solution.py:24
  595.0 37.1 %collective-permute-start.5 = (f32[256,768]{1,0:T(8,128)S(1)}, f32[256,768]{1,0:T(8,128)S(1)}, u32[]{:S(2)}, u32[]{:S(2)}) collective-permute-start(f32[256,768]{1,0:T(8,128)S(1)} %multiply_select_fusion.1), channel_id=1, source_target_pairs={{0,4},{1,5},{2,6},{3,7},{4,0},{5,1},{6,2},{7,3},{8,12},{9,13},{10,... | collective-permute-start | bytes 2359304 | tf_op jit(solution)/shard_map/ppermute | solution.py:24
  650.4 280.6 %reduce-scatter.12.cloned.1.call-start = ((), (), s32[]{:S(2)}) async-start(), calls=%async_computation.12 | async-start | bytes 15925248 | tf_op jit(solution)/shard_map/reduce_scatter | solution.py:232
  683.9 88.0 %copy-start.3 = (bf16[512,768]{1,0:T(8,128)(2,1)S(1)}, bf16[512,768]{1,0:T(8,128)(2,1)}, u32[]{:S(2)}) copy-start(bf16[512,768]{1,0:T(8,128)(2,1)} %param.22) | copy-start | bytes 2359300
  683.9 86.7 %collective-permute-start.6 = (bf16[2,512,768]{1,2,0:T(8,128)(2,1)S(1)}, bf16[2,512,768]{1,2,0:T(8,128)(2,1)S(1)}, u32[]{:S(2)}, u32[]{:S(2)}) collective-permute-start(bf16[2,512,768]{1,2,0:T(8,128)(2,1)S(1)} %pad_maximum_fusion.4), channel_id=1, source_target_pairs={{0,4},{1,5},{2,6},{3,7},{4,0},{5,1},{6,2},{7,3},{8,12},{9,13},{10,... | collective-permute-start | bytes 4718600 | tf_op jit(solution)/shard_map/ppermute | solution.py:24
  685.1 85.7 %copy-start.17 = (bf16[12,64,512]{2,1,0:T(8,128)(2,1)}, bf16[12,64,512]{2,1,0:T(8,128)(2,1)S(1)}, u32[]{:S(2)}) copy-start(bf16[12,64,512]{2,1,0:T(8,128)(2,1)S(1)} %multiply_convert_fusion.3) | copy-start | bytes 2359300
  788.1 331.5 %reduce-scatter.20.cloned.1.call-start = ((), (), s32[]{:S(2)}) async-start(), calls=%async_computation.16 | async-start | bytes 21233664 | tf_op jit(solution)/shard_map/reduce_scatter | solution.py:235
  800.5 507.9 %reduce-scatter.16.cloned.1.call-start = ((), (), s32[]{:S(2)}) async-start(), calls=%async_computation.14 | async-start | bytes 21233664 | tf_op jit(solution)/shard_map/reduce_scatter | solution.py:234
  812.5 546.3 %reduce-scatter.24.cloned.1.call-start = ((), (), s32[]{:S(2)}) async-start(), calls=%async_computation.18 | async-start | bytes 983040
  815.5 561.5 %reduce-scatter.22.cloned.1.call-start = ((), (), s32[]{:S(2)}) async-start(), calls=%async_computation.17 | async-start | bytes 2949120
  939.1 515.0 %all-reduce.11.cloned.1.call-start = ((), (), s32[]{:S(2)}) async-start(), calls=%async_computation.19 | async-start | bytes 4718592
  1125.0 183.4 %copy-start.43 = (u32[32]{0:T(128)S(1)}, u32[32]{0:T(128)}, u32[]{:S(2)}) copy-start(u32[32]{0:T(128)} %constant.216) | copy-start | bytes 388
  1125.0 184.7 %copy-start.4 = (bf16[512,768]{1,0:T(8,128)(2,1)S(1)}, bf16[512,768]{1,0:T(8,128)(2,1)}, u32[]{:S(2)}) copy-start(bf16[512,768]{1,0:T(8,128)(2,1)} %param.22) | copy-start | bytes 2359300
  1125.0 184.7 %copy-start.18 = (bf16[12,64,512]{2,1,0:T(8,128)(2,1)S(1)}, bf16[12,64,512]{2,1,0:T(8,128)(2,1)}, u32[]{:S(2)}) copy-start(bf16[12,64,512]{2,1,0:T(8,128)(2,1)} %copy-done.17) | copy-start | bytes 2359300
  1125.0 369.8 %reduce-scatter.18.cloned.1.call-start = ((), (), s32[]{:S(2)}) async-start(), calls=%async_computation.15 | async-start | bytes 2949120 | tf_op jit(solution)/shard_map/reduce_scatter | solution.py:240
  1361.1 94.3 %copy-start.21 = (f32[2,384,192]{1,2,0:T(8,128)S(1)}, f32[2,384,192]{1,2,0:T(8,128)}, u32[]{:S(2)}) copy-start(f32[2,384,192]{1,2,0:T(8,128)} %param.36) | copy-start | bytes 1769476
  1361.1 94.3 %copy-start.31 = (f32[2,384,192]{1,2,0:T(8,128)S(1)}, f32[2,384,192]{1,2,0:T(8,128)}, u32[]{:S(2)}) copy-start(f32[2,384,192]{1,2,0:T(8,128)} %param.37) | copy-start | bytes 1769476
  1361.1 94.3 %copy-start.32 = (f32[2,384,192]{1,2,0:T(8,128)S(1)}, f32[2,384,192]{1,2,0:T(8,128)}, u32[]{:S(2)}) copy-start(f32[2,384,192]{1,2,0:T(8,128)} %param.38) | copy-start | bytes 1769476
  1378.7 116.1 %copy-start.22 = (f32[2,96,768]{2,1,0:T(8,128)S(1)}, f32[2,96,768]{2,1,0:T(8,128)}, u32[]{:S(2)}) copy-start(f32[2,96,768]{2,1,0:T(8,128)} %param.33) | copy-start | bytes 1769476
  1381.3 113.5 %copy-start.33 = (f32[2,96,768]{2,1,0:T(8,128)S(1)}, f32[2,96,768]{2,1,0:T(8,128)}, u32[]{:S(2)}) copy-start(f32[2,96,768]{2,1,0:T(8,128)} %param.34) | copy-start | bytes 1769476
  (39 other events, 710.3 us)
Sparse Core Ops, SparseCore 0:
  10.5 30.4 all-gather.7
  43.4 27.7 all-gather.11
  73.3 33.6 all-gather.5
  108.5 207.3 all-gather.9
  317.3 132.1 all-gather.13
  650.5 70.5 reduce-scatter.13
  788.3 142.6 reduce-scatter.11
  933.3 186.2 reduce-scatter.19
  1122.0 186.3 reduce-scatter.15
  1311.1 24.7 reduce-scatter.23
  1339.0 37.9 reduce-scatter.21
  1380.0 74.0 all-reduce.10
  1457.4 37.3 reduce-scatter.17
